TPU v7x, 1024 devices: a whole 4x4x32 slice. The times are simulated.
1024 devices in a mesh: blk: 64 (over z_hi, x, y), grp: 16 (over z_lo, core).
Axes of the slice: x: 4, y: 4, z: 32 (z_hi: 4, z_lo: 8; z = z_hi * 8 + z_lo), core: 2. Of those that a mesh axis runs over, the one named last changes fastest.
Arguments:
- pooled_picture_vectors: bfloat16 [8192, 1536], P(('blk', 'grp')), may hold values from -6 to 6
- picture_mapping_matrix: bfloat16 [1536, 1152], replicated, may hold values from -0.15625 to 0.15625
- caption_vectors: bfloat16 [8192, 1152], P(('blk', 'grp')), may hold values from -6 to 6
- matching_caption_slot: int32 [8192], P(('blk', 'grp')), may hold values from 0 to 8191, each once
- picture_instance_class: int32 [8192], P(('blk', 'grp')), may hold values from 0 to 15
- caption_instance_class: int32 [8192], P(('blk', 'grp')), may hold values from 0 to 15
- score_scale: float32 [1], replicated, may hold values from 5 to 12
- score_offset: float32 [1], replicated, may hold values from -3 to -1
Outputs:
- image_grad: bfloat16 [8192, 1536], P(('blk', 'grp'))
- text_grad: bfloat16 [8192, 1152], P(('blk', 'grp'))
Inputs may be any that keep to these rules, and one draw needn't show every extreme that they name: `matching_caption_slot`: every text is the positive of exactly one image.
All inputs are finite; a program needn't handle non-finite values.
Results may differ from a plain program's by a relative error of at most 0.028.
Values may be sent and summed in bfloat16 or wider, within the bound.
A program may use at most 32 MiB of HBM per device.

v0:
```python
import jax
import jax.numpy as jnp
from jax import lax
from jax.sharding import PartitionSpec as P

epsilon = 1e-06


def normalize(values):
    norm_rows = jnp.sqrt(jnp.sum(values * values, axis=1, keepdims=True) + epsilon)
    return (values / norm_rows, norm_rows)


def body(
    pooled_picture_vectors,
    picture_mapping_matrix,
    caption_vectors,
    matching_caption_slot,
    picture_instance_class,
    caption_instance_class,
    score_scale,
    score_offset,
):
    shard_rows = caption_vectors.shape[0]
    group_count = lax.axis_size("grp")
    embedded = jnp.dot(
        pooled_picture_vectors, picture_mapping_matrix, preferred_element_type=jnp.float32
    )
    image_dir, image_norm = normalize(embedded)
    image_unit = image_dir.astype(jnp.bfloat16)
    text_dir, text_norm = normalize(caption_vectors.astype(jnp.float32))
    caption_direction = text_dir.astype(jnp.bfloat16)
    block_unit, block_pair, block_group = (
        lax.all_gather(image_unit, "grp", axis=0, tiled=True),
        lax.all_gather(matching_caption_slot, "grp", axis=0, tiled=True),
        lax.all_gather(picture_instance_class, "grp", axis=0, tiled=True),
    )
    scaled_score_factor = score_scale[0]
    offset_amount = score_offset[0]
    column = lax.axis_index("grp") * shard_rows
    all_unit, all_group = (
        lax.all_gather(caption_direction, "blk", axis=0, tiled=True),
        lax.all_gather(caption_instance_class, "blk", axis=0, tiled=True),
    )
    how_many = all_unit.shape[0]
    position = jnp.arange(how_many, dtype=jnp.int32)
    text_index = (
        position // shard_rows * (shard_rows * group_count) + column + position % shard_rows
    )
    similarity_scores = (
        lax.dot_general(
            block_unit, all_unit, (((1,), (1,)), ((), ())), preferred_element_type=jnp.float32
        )
        * scaled_score_factor
        + offset_amount
    )
    positive = block_pair[:, None] == text_index[None, :]
    match_sign = jnp.where(positive, 1.0, -1.0).astype(jnp.float32)
    same = block_group[:, None] == all_group[None, :]
    retained_match_mask = jnp.where(same & jnp.logical_not(positive), 0.0, 1.0).astype(jnp.float32)
    loss_weight_factor = (
        -retained_match_mask
        * match_sign
        * jax.nn.sigmoid(-match_sign * similarity_scores)
        * scaled_score_factor
    ).astype(jnp.bfloat16)
    image_piece = jnp.dot(loss_weight_factor, all_unit, preferred_element_type=jnp.float32)
    loss_weight_factor, image_part = (loss_weight_factor, image_piece)
    text_partial = lax.dot_general(
        loss_weight_factor, block_unit, (((0,), (0,)), ((), ())), preferred_element_type=jnp.float32
    )
    text_unit_grad = lax.psum_scatter(text_partial, "blk", scatter_dimension=0, tiled=True)
    image_unit_grad = lax.psum_scatter(
        image_part.astype(jnp.bfloat16), "grp", scatter_dimension=0, tiled=True
    ).astype(jnp.float32)
    inner = jnp.sum(image_dir * image_unit_grad, axis=1, keepdims=True)
    embed_grad = ((image_unit_grad - image_dir * inner) / image_norm).astype(jnp.bfloat16)
    image_grad = lax.dot_general(
        embed_grad,
        picture_mapping_matrix,
        (((1,), (1,)), ((), ())),
        preferred_element_type=jnp.float32,
    ).astype(jnp.bfloat16)
    text_inner = jnp.sum(text_dir * text_unit_grad, axis=1, keepdims=True)
    text_grad = ((text_unit_grad - text_dir * text_inner) / text_norm).astype(jnp.bfloat16)
    return (image_grad, text_grad)


def solution(mesh):
    placed = (
        P(("blk", "grp"), None),
        P(),
        P(("blk", "grp"), None),
        P(("blk", "grp")),
        P(("blk", "grp")),
        P(("blk", "grp")),
        P(),
        P(),
    )
    return jax.shard_map(
        body,
        mesh=mesh,
        in_specs=placed,
        out_specs=(P(("blk", "grp"), None), P(("blk", "grp"), None)),
        check_vma=False,
    )
```

profile of v0, /device:TPU:8, one launch (start us, length us, event | category | flops | bytes accessed | tf_op | source)
XLA Modules:
  0.0 1572.8 jit_solution(1661372059758024759)
XLA Ops:
  7.2 0.0 copy-start
  7.2 0.0 all-gather.2.cloned.1.call-start
  7.2 1.0 fusion.10
  8.2 1.4 fusion.29
  9.7 0.0 all-gather.2.cloned.1.call-update
  9.7 0.0 all-reduce.9.cloned.1.call-start
  11.0 1.5 fusion.31
  13.7 0.9 dynamic-update-slice.2
  14.6 0.8 dynamic-update-slice
  15.4 0.8 dynamic-update-slice.1
  16.3 19.5 %all-reduce.5 = (s32[128]{0:T(128)}, s32[128]{0:T(128)}) all-reduce(s32[128]{0:T(128)S(1)} %dynamic-update-slice.2, s32[128]{0:T(128)S(1)} %dynamic-update-slice), channel_id=1, replica_groups=mesh['blk'=64,'grp'=16] {'grp'}, use_global_device_ids=true, to_apply=%add.2 | all-reduce | flops 256 | bytes 2048
  35.8 42.5 %all-reduce.1 = s32[512]{0:T(512)S(1)} all-reduce(s32[512]{0:T(512)S(1)} %dynamic-update-slice.1), channel_id=1, replica_groups=mesh['blk'=64,'grp'=16] {'blk'}, use_global_device_ids=true, to_apply=%add.1 | all-reduce | flops 512 | bytes 4096
  78.3 0.0 copy-done
  78.3 1.4 multiply_reduce_fusion.1
  79.7 0.0 copy-start.2
  79.8 0.6 copy-done.2
  80.3 0.1 fusion.30
  80.4 32.4 %all_gather.18 = bf16[128,1152]{1,0:T(8,128)(2,1)} all-gather(bf16[8,1152]{1,0:T(8,128)(2,1)S(1)} %fusion.30), channel_id=1, replica_groups=mesh['blk'=64,'grp'=16] {'grp'}, dimensions={0}, use_global_device_ids=true | all-gather | bytes 313344 | tf_op jit(solution)/shard_map/all_gather | solution.py:34
  112.8 76.3 %all-gather.2.cloned.1.call-done = bf16[512,1152]{1,0:T(8,128)(2,1)} async-done(((bf16[8,1152]{1,0:T(8,128)(2,1)}), bf16[512,1152]{1,0:T(8,128)(2,1)}) %all-gather.2.cloned.1.call-update) | async-done | bytes 1179664 | tf_op jit(solution)/shard_map/all_gather | solution.py:42
  189.1 0.0 copy-start.1
  189.1 2.0 fusion.8
  191.2 0.0 copy-start.3
  191.2 0.6 copy-done.3
  191.8 0.0 copy-done.1
  191.8 1.1 convolution_convert_fusion
  192.9 0.0 all-reduce.9.cloned.1.call-update
  192.9 0.0 all-reduce.11.cloned.1.call-start
  193.0 2.9 fusion.33
  195.9 0.0 all-reduce.11.cloned.1.call-update
  197.2 194.1 %all-reduce.9.cloned.1.call-done = bf16[128,1152]{1,0:T(8,128)(2,1)} async-done(((bf16[128,1152]{1,0:T(8,128)(2,1)}), bf16[128,1152]{1,0:T(8,128)(2,1)}) %all-reduce.9.cloned.1.call-update) | async-done | bytes 294928
  391.3 1.0 fusion.11
  392.3 2.4 convolution_convert_fusion.1
  394.7 1169.0 %all-reduce.11.cloned.1.call-done = f32[512,1152]{1,0:T(8,128)} async-done(((f32[512,1152]{1,0:T(8,128)}), f32[512,1152]{1,0:T(8,128)}) %all-reduce.11.cloned.1.call-update) | async-done | bytes 2359312
  1563.8 1.0 multiply_reduce_fusion
  1564.8 1.5 divide_convert_fusion
  (6 shorter events, 0.0 us)
Async XLA Ops:
  7.2 71.2 %copy-start = (bf16[1536,1152]{1,0:T(8,128)(2,1)S(1)}, bf16[1536,1152]{1,0:T(8,128)(2,1)}, u32[]{:S(2)}) copy-start(bf16[1536,1152]{1,0:T(8,128)(2,1)} %param.9) | copy-start | bytes 10616836
  7.2 182.0 %all-gather.2.cloned.1.call-start = ((), (), s32[]{:S(2)}) async-start(), calls=%async_computation | async-start | bytes 1198080 | tf_op jit(solution)/shard_map/all_gather | solution.py:42
  9.7 381.7 %all-reduce.9.cloned.1.call-start = ((), (), s32[]{:S(2)}) async-start(), calls=%async_computation.1 | async-start | bytes 589824
  79.7 0.6 copy-start.2
  189.1 2.7 copy-start.1
  191.2 0.6 copy-start.3
  192.9 1370.9 %all-reduce.11.cloned.1.call-start = ((), (), s32[]{:S(2)}) async-start(), calls=%async_computation.2 | async-start | bytes 4718592
Sparse Core Ops, SparseCore 0:
  14.4 174.7 all-gather.1
  193.0 198.2 all-reduce.8
  395.3 1168.4 all-reduce.10
where the time goes:
time: 1570 us
  waiting for transfers between devices  1440 us (92%)
  blocking collectives  94.4 us (6%)
  between operations  17.6 us (1%)
    unnamed x5, waiting for transfers between devices  1360 us
    all_gather x1, waiting for transfers between devices, body(): lax.all_gather(caption_direction, 'blk', axis=0, tiled=True)  76.3 us
    unnamed x2, blocking collectives  62 us
    all_gather x1, blocking collectives, body(): lax.all_gather(image_unit, 'grp', axis=0, tiled=True)  32.4 us
  transfers between devices with their start and end apart: 3, of which 3 were waited for; matrix products, arithmetic and copies ran while one was open for 1% of the time, Pallas kernels for 0%

commit v1 on v0

v1 whole, which is shorter than its diff:
```python
import jax
import jax.numpy as jnp
from jax import lax
from jax.experimental import pallas as pl
from jax.experimental.pallas import tpu as pltpu
from jax.sharding import PartitionSpec as P

epsilon = 1e-06
D = 1152
FEATS = 1536
ROWS = 8
TILES = D // 128
FOLD = (TILES + 1) * ROWS
MESH = pl.DeviceIdType.MESH

IMAGE_Z = tuple(range(-4, 4))
TEXT_Z = (-12, -4, 4, 12)
IMAGE_XY = ((0, 0), (1, 0), (0, 1), (1, 1))
TEXT_XY = ((1, 1), (1, -1), (-1, 1), (-1, -1))
OWN_Z = IMAGE_Z.index(0)


def fold(rows):
    pieces = [rows[:, 128 * t : 128 * (t + 1)] for t in range(TILES)]
    pieces.append(jnp.zeros((ROWS, 128), jnp.float32))
    return jnp.concatenate(pieces, axis=0).astype(jnp.bfloat16)


def unfold(block):
    return jnp.concatenate([block[ROWS * t : ROWS * (t + 1)] for t in range(TILES)], axis=1)


def normalize(values):
    norm_rows = jnp.sqrt(jnp.sum(values * values, axis=1, keepdims=True) + epsilon)
    return values / norm_rows, norm_rows


def column(ref, row, shift, mask):
    out = jnp.zeros((ROWS, 128), jnp.int32)
    for r in range(ROWS):
        out = jnp.where(row == r, lax.bitwise_and(lax.shift_right_logical(ref[r], shift), mask), out)
    return out


def kernel(
    scale_ref, offset_ref, slot_ref, iclass_ref, tclass_ref, pooled_ref, caption_ref, w_hbm,
    image_out, text_out,
    w_ref, img, ztxt, txt, x_ref, y_ref, mx_ref, my_ref,
    ig_ref, tg_ref, s_out, s_in, p_txt, p_txt_in, p_img, p_img_in, z_txt, z_txt_in, z_img, z_img_in, o_txt,
    w_sem, send, recv,
):
    blk = lax.axis_index("blk")
    grp = lax.axis_index("grp")
    x, y, z, core = (blk // 4) % 4, blk % 4, (blk // 16) * 8 + grp // 2, grp % 2
    sign = 1 - 2 * core

    def device(dx=0, dy=0, dz=0, other=False):
        to_x, to_y, to_z = (x + dx + 4) % 4, (y + dy + 4) % 4, (z + dz + 32) % 32
        to_core = 1 - core if other else core
        return ((to_z // 8) * 16 + to_x * 4 + to_y, (to_z % 8) * 2 + to_core)

    partners = [dict(other=True)]
    partners += [dict(dz=d) for d in (-12, 12, -4, 4, -3, 3, -2, 2, -1, 1)]
    partners += [dict(dx=dx, dy=dy) for dx in (-1, 0, 1) for dy in (-1, 0, 1) if dx or dy]
    barrier = pltpu.get_barrier_semaphore()
    for p in partners:
        pl.semaphore_signal(barrier, inc=1, device_id=device(**p), device_id_type=MESH)

    w_copy = pltpu.make_async_copy(w_hbm, w_ref, w_sem)
    w_copy.start()

    row = lax.broadcasted_iota(jnp.int32, (ROWS, 128), 0)
    lane = lax.broadcasted_iota(jnp.int32, (ROWS, 128), 1)

    text_dir, text_norm = normalize(caption_ref[...].astype(jnp.float32))
    text_label = jnp.where(lane == 0, column(tclass_ref, row, 0, 15), jnp.where(lane == 1, blk, grp * ROWS + row))
    own_text = jnp.concatenate(
        [text_dir[:, 128 * t : 128 * (t + 1)] for t in range(TILES)] + [text_label.astype(jnp.float32)], axis=0
    )
    s_out[0] = own_text.astype(jnp.bfloat16)

    w_copy.wait()
    embedded = jnp.dot(pooled_ref[...], w_ref[...], preferred_element_type=jnp.float32)
    image_dir, image_norm = normalize(embedded)
    image_label = jnp.where(
        lane == 0, column(iclass_ref, row, 0, 15),
        jnp.where(lane == 1, column(slot_ref, row, 7, 63), column(slot_ref, row, 0, 127)),
    )
    own_image = jnp.concatenate(
        [image_dir[:, 128 * t : 128 * (t + 1)] for t in range(TILES)] + [image_label.astype(jnp.float32)], axis=0
    )
    img[0, OWN_Z] = own_image.astype(jnp.bfloat16)

    pl.semaphore_wait(barrier, len(partners))

    count = [0]

    def copy(src, dst, **to):
        n = count[0]
        count[0] += 1
        c = pltpu.make_async_remote_copy(
            src_ref=src, dst_ref=dst, send_sem=send.at[n], recv_sem=recv.at[n],
            device_id=device(**to), device_id_type=MESH,
        )
        c.start()
        return c

    def arrive(copies):
        for c in copies:
            c.wait_recv()

    started = []
    stage_t = [copy(s_out.at[0], ztxt.at[n], dz=-b) for n, b in enumerate(TEXT_Z)]
    stage_i = [
        copy(img.at[0, OWN_Z], img.at[0, n], dz=-sign * k) for n, k in enumerate(IMAGE_Z) if k
    ]
    started += stage_t + stage_i
    arrive(stage_i)
    plane_i = [
        copy(img.at[0], img.at[q], dx=-sign * ax, dy=-sign * ay) for q, (ax, ay) in enumerate(IMAGE_XY) if q
    ]
    arrive(stage_t)
    plane_t = [copy(ztxt, txt.at[0, q], dx=-bx, dy=-by) for q, (bx, by) in enumerate(TEXT_XY)]
    started += plane_i + plane_t
    arrive(plane_t)
    across = copy(txt.at[0], txt.at[1], other=True)
    started.append(across)

    def spread(block_of, dst, label, n):
        a, b = block_of(2 * n).astype(jnp.float32), block_of(2 * n + 1).astype(jnp.float32)
        at = pl.ds(pl.multiple_of(16 * n, 16), 16)
        dst[at, :] = jnp.concatenate([unfold(a), unfold(b)], axis=0).astype(jnp.bfloat16)
        label[at, :] = jnp.concatenate([a[ROWS * TILES :], b[ROWS * TILES :]], axis=0).astype(jnp.bfloat16)

    arrive(plane_i)
    for n in range(16):
        spread(lambda j: img[j // 8, j % 8], x_ref, mx_ref, n)
    for n in range(8):
        spread(lambda j: txt[0, j // 4, j % 4], y_ref, my_ref, n)
    arrive([across])
    for n in range(8, 16):
        spread(lambda j: txt[1, (j - 16) // 4, j % 4], y_ref, my_ref, n)

    scale, offset = scale_ref[0], offset_ref[0]
    nt = (((1,), (1,)), ((), ()))
    scores = lax.dot_general(x_ref[...], y_ref[...], nt, preferred_element_type=jnp.float32) * scale + offset
    pick_row = lax.broadcasted_iota(jnp.int32, (ROWS, 128), 0)
    basis = jnp.where(
        pick_row == 0, jnp.where(lane == 0, 1.0, 0.0),
        jnp.where(pick_row == 1, jnp.where(lane == 1, 128.0, jnp.where(lane == 2, 1.0, 0.0)), 0.0),
    ).astype(jnp.bfloat16)
    text_rows = lax.dot_general(basis, my_ref[...], nt, preferred_element_type=jnp.float32)
    image_columns = lax.dot_general(mx_ref[...], basis, nt, preferred_element_type=jnp.float32)
    positive = image_columns[:, 1:2] == text_rows[1:2, :]
    same = image_columns[:, 0:1] == text_rows[0:1, :]
    sigmoid = 1.0 / (1.0 + jnp.exp(jnp.where(positive, scores, -scores)))
    signed = jnp.where(positive, -scale, jnp.where(same, 0.0, scale))
    weight = (sigmoid * signed).astype(jnp.bfloat16)

    tg_ref[...] = lax.dot_general(
        weight, x_ref[...], (((0,), (0,)), ((), ())), preferred_element_type=jnp.float32
    )
    for n in range(16):
        s_in[n] = fold(tg_ref[128 + 8 * n : 136 + 8 * n, :])
    back_across = copy(s_in, p_txt, other=True)
    ig_ref[...] = jnp.dot(weight, y_ref[...], preferred_element_type=jnp.float32)
    for n in range(32):
        p_img[n // 8, n % 8] = fold(ig_ref[8 * n : 8 * n + 8, :])
    back_i = [
        copy(p_img.at[q], p_img_in.at[q], dx=sign * ax, dy=sign * ay) for q, (ax, ay) in enumerate(IMAGE_XY) if q
    ]
    arrive([back_across])
    for n in range(16):
        mine = fold(tg_ref[8 * n : 8 * n + 8, :]).astype(jnp.float32)
        z_txt[n] = (mine + p_txt[n].astype(jnp.float32)).astype(jnp.bfloat16)
    back_t = [copy(z_txt.at[pl.ds(4 * q, 4)], p_txt_in.at[q], dx=bx, dy=by) for q, (bx, by) in enumerate(TEXT_XY)]
    started += [back_across] + back_i + back_t

    arrive(back_i)
    home_i = []
    for n, k in enumerate(IMAGE_Z):
        total = p_img[0, n].astype(jnp.float32)
        for q in range(1, 4):
            total += p_img_in[q, n].astype(jnp.float32)
        z_img[n] = total.astype(jnp.bfloat16)
        if k:
            home_i.append(copy(z_img.at[n], z_img_in.at[n], dz=sign * k))
    arrive(back_t)
    home_t = []
    for n, b in enumerate(TEXT_Z):
        total = p_txt_in[0, n].astype(jnp.float32)
        for q in range(1, 4):
            total += p_txt_in[q, n].astype(jnp.float32)
        o_txt[n] = total.astype(jnp.bfloat16)
        home_t.append(copy(o_txt.at[n], z_txt_in.at[n], dz=b))
    started += home_i + home_t

    arrive(home_i)
    total = z_img[OWN_Z].astype(jnp.float32)
    for n, k in enumerate(IMAGE_Z):
        if k:
            total += z_img_in[n].astype(jnp.float32)
    grad = unfold(total)
    inner = jnp.sum(image_dir * grad, axis=1, keepdims=True)
    embed_grad = ((grad - image_dir * inner) / image_norm).astype(jnp.bfloat16)
    image_out[...] = lax.dot_general(embed_grad, w_ref[...], nt, preferred_element_type=jnp.float32).astype(
        jnp.bfloat16
    )
    arrive(home_t)
    total = z_txt_in[0].astype(jnp.float32)
    for n in range(1, 4):
        total += z_txt_in[n].astype(jnp.float32)
    grad = unfold(total)
    inner = jnp.sum(text_dir * grad, axis=1, keepdims=True)
    text_out[...] = ((grad - text_dir * inner) / text_norm).astype(jnp.bfloat16)
    for c in started:
        c.wait_send()


def body(
    pooled_picture_vectors,
    picture_mapping_matrix,
    caption_vectors,
    matching_caption_slot,
    picture_instance_class,
    caption_instance_class,
    score_scale,
    score_offset,
):
    smem = pl.BlockSpec(memory_space=pltpu.SMEM)
    vmem = pl.BlockSpec(memory_space=pltpu.VMEM)
    half = jnp.bfloat16
    return pl.pallas_call(
        kernel,
        out_shape=(
            jax.ShapeDtypeStruct((ROWS, FEATS), half),
            jax.ShapeDtypeStruct((ROWS, D), half),
        ),
        in_specs=[smem] * 5 + [vmem] * 2 + [pl.BlockSpec(memory_space=pl.ANY)],
        out_specs=(vmem, vmem),
        scratch_shapes=[
            pltpu.VMEM((FEATS, D), half),
            pltpu.VMEM((4, 8, FOLD, 128), half),
            pltpu.VMEM((4, FOLD, 128), half),
            pltpu.VMEM((2, 4, 4, FOLD, 128), half),
            pltpu.VMEM((256, D), half),
            pltpu.VMEM((256, D), half),
            pltpu.VMEM((256, 128), half),
            pltpu.VMEM((256, 128), half),
            pltpu.VMEM((256, D), jnp.float32),
            pltpu.VMEM((256, D), jnp.float32),
            pltpu.VMEM((1, FOLD, 128), half),
            pltpu.VMEM((16, FOLD, 128), half),
            pltpu.VMEM((16, FOLD, 128), half),
            pltpu.VMEM((4, 4, FOLD, 128), half),
            pltpu.VMEM((4, 8, FOLD, 128), half),
            pltpu.VMEM((4, 8, FOLD, 128), half),
            pltpu.VMEM((16, FOLD, 128), half),
            pltpu.VMEM((4, FOLD, 128), half),
            pltpu.VMEM((8, FOLD, 128), half),
            pltpu.VMEM((8, FOLD, 128), half),
            pltpu.VMEM((4, FOLD, 128), half),
            pltpu.SemaphoreType.DMA,
            pltpu.SemaphoreType.DMA((40,)),
            pltpu.SemaphoreType.DMA((40,)),
        ],
        compiler_params=pltpu.CompilerParams(
            collective_id=0, has_side_effects=True, vmem_limit_bytes=40 * 2**20
        ),
        name="contrast",
    )(
        score_scale, score_offset, matching_caption_slot, picture_instance_class, caption_instance_class,
        pooled_picture_vectors, caption_vectors, picture_mapping_matrix,
    )


def solution(mesh):
    placed = (
        P(("blk", "grp"), None),
        P(),
        P(("blk", "grp"), None),
        P(("blk", "grp")),
        P(("blk", "grp")),
        P(("blk", "grp")),
        P(),
        P(),
    )
    return jax.shard_map(
        body,
        mesh=mesh,
        in_specs=placed,
        out_specs=(P(("blk", "grp"), None), P(("blk", "grp"), None)),
        check_vma=False,
    )
```

time: 1570 us -> 87.2 us (0.06)
  the two profiles are of different devices: /device:TPU:8 before, /device:TPU:25 now
where the time goes in v1:
time: 87.2 us; the launch traced here: 86.9 us
  Pallas kernels  78.3 us (90%)
  local copies, waits for them, and re-layouts  6.63 us (8%)
  between operations  1.95 us (2%)
    pallas_call x1, Pallas kernels, body(): pl.pallas_call(kernel, out_shape=(jax.ShapeDtypeStruct((ROWS, FEATS), hal...  78.3 us
    unnamed x14, local copies, waits for them, and re-layouts  6.63 us

profile of v1, /device:TPU:25, one launch (start us, length us, event | category | flops | bytes accessed | tf_op | source)
XLA Modules:
  0.0 86.9 jit_solution(11984143709559685078)
XLA Ops:
  1.9 0.0 copy-start
  1.9 2.0 %copy-done = bf16[1536,1152]{1,0:T(8,128)(2,1)S(1)} copy-done((bf16[1536,1152]{1,0:T(8,128)(2,1)S(1)}, bf16[1536,1152]{1,0:T(8,128)(2,1)}, u32[]{:S(2)}) %copy-start) | copy-done | bytes 3538968
  3.9 0.0 copy-start.1
  3.9 0.7 copy-done.1
  4.7 0.0 copy-start.2
  4.7 0.7 copy-done.2
  5.4 0.0 copy-start.3
  5.4 0.7 copy-done.3
  6.0 0.0 copy-start.4
  6.0 0.7 copy-done.4
  6.7 0.0 copy-start.5
  6.7 0.7 copy-done.5
  7.4 78.3 %contrast.1 = (bf16[8,1536]{1,0:T(8,128)(2,1)S(1)}, bf16[8,1152]{1,0:T(8,128)(2,1)S(1)}) custom-call(f32[1]{0:T(128)S(6)} %copy.12.scale_ref, f32[1]{0:T(128)S(6)} %copy.13.offset_ref, s32[8]{0:T(128)S(1)} %copy-done.3, s32[8]{0:T(128)S(1)} %copy-done.4, s32[8]{0:T(128)S(1)} %copy-done.5, bf16[8,1536]{1,0:T(8,128)(2,1)S(1)} %copy-done.1, ...), custom_call_target="tpu_custom_call" | custom-call | tf_op jit(solution)/shard_map/contrast/pallas_call | solution.py:233
  85.7 0.6 copy.14
  86.3 0.6 copy.15
Async XLA Ops:
  1.9 2.0 %copy-start = (bf16[1536,1152]{1,0:T(8,128)(2,1)S(1)}, bf16[1536,1152]{1,0:T(8,128)(2,1)}, u32[]{:S(2)}) copy-start(bf16[1536,1152]{1,0:T(8,128)(2,1)} %w_hbm.1) | copy-start | bytes 10616836
  3.9 0.7 copy-start.1
  4.7 0.7 copy-start.2
  5.4 0.7 copy-start.3
  6.0 0.7 copy-start.4
  6.7 0.7 copy-start.5

commit v2 on v1

v2 whole, which is shorter than its diff:
```python
import jax
import jax.numpy as jnp
from jax import lax
from jax.experimental import pallas as pl
from jax.experimental.pallas import tpu as pltpu
from jax.sharding import PartitionSpec as P

epsilon = 1e-06
D = 1152
FEATS = 1536
ROWS = 8
TILES = D // 128
FOLD = (TILES + 1) * ROWS
MESH = pl.DeviceIdType.MESH

IMAGE_Z = ((0, -1), (1, -2), (2, -3), (3, -4))
TEXT_Z = ((-4, 4), (-12, 12))
IMAGE_XY = ((0, 0), (1, 0), (0, 1), (1, 1))
TEXT_XY = ((1, 1), (1, -1), (-1, 1), (-1, -1))
CHUNKS = 3
NT = (((1,), (1,)), ((), ()))
TN = (((0,), (0,)), ((), ()))


def fold(rows):
    pieces = [rows[:, 128 * t : 128 * (t + 1)] for t in range(TILES)]
    pieces.append(jnp.zeros((ROWS, 128), jnp.float32))
    return jnp.concatenate(pieces, axis=0).astype(jnp.bfloat16)


def unfold(block):
    return jnp.concatenate([block[ROWS * t : ROWS * (t + 1)] for t in range(TILES)], axis=1)


def normalize(values):
    norm_rows = jnp.sqrt(jnp.sum(values * values, axis=1, keepdims=True) + epsilon)
    return values / norm_rows, norm_rows


def column(ref, row, shift, mask):
    out = jnp.zeros((ROWS, 128), jnp.int32)
    for r in range(ROWS):
        out = jnp.where(row == r, lax.bitwise_and(lax.shift_right_logical(ref[r], shift), mask), out)
    return out


def kernel(
    scale_ref, offset_ref, slot_hbm, iclass_hbm, tclass_hbm, pooled_hbm, caption_hbm, w_hbm,
    image_out, text_out,
    slot_ref, iclass_ref, tclass_ref, pooled_ref, caption_ref, w_ref, wt_ref,
    own_text, img, ztxt, via, txt, x_ref, y_ref, mx_ref, my_ref, tg_ref, ig_ref,
    r0, r0_in, rt1, rt1_in, rt2, rt2_in, ri1, ri1_in, ri2, ri2_in,
    load, send, recv,
):
    blk = lax.axis_index("blk")
    grp = lax.axis_index("grp")
    x, y, z, core = (blk // 4) % 4, blk % 4, (blk // 16) * 8 + grp // 2, grp % 2
    sign = 1 - 2 * core

    def device(dx=0, dy=0, dz=0, other=False):
        to_x, to_y, to_z = (x + dx + 4) % 4, (y + dy + 4) % 4, (z + dz + 32) % 32
        to_core = 1 - core if other else core
        return ((to_z // 8) * 16 + to_x * 4 + to_y, (to_z % 8) * 2 + to_core)

    rows_w = FEATS // CHUNKS
    loads = [
        pltpu.make_async_copy(src, dst, load.at[n])
        for n, (src, dst) in enumerate(
            [(caption_hbm, caption_ref), (tclass_hbm, tclass_ref), (pooled_hbm, pooled_ref)]
            + [(w_hbm.at[pl.ds(rows_w * n, rows_w)], w_ref.at[pl.ds(rows_w * n, rows_w)]) for n in range(CHUNKS)]
            + [(iclass_hbm, iclass_ref), (slot_hbm, slot_ref)]
        )
    ]
    for c in loads:
        c.start()
    partners = [dict(dz=d) for d in (-4, 4, -3, 3, -2, 2, -1, 1)]
    partners += [dict(dx=dx, dy=dy) for dx in (-1, 0, 1) for dy in (-1, 0, 1) if dx or dy]
    partners += [dict(other=True)]
    barrier = pltpu.get_barrier_semaphore()
    for p in partners:
        pl.semaphore_signal(barrier, inc=1, device_id=device(**p), device_id_type=MESH)

    row = lax.broadcasted_iota(jnp.int32, (ROWS, 128), 0)
    lane = lax.broadcasted_iota(jnp.int32, (ROWS, 128), 1)

    def block_of(values, label):
        pieces = [values[:, 128 * t : 128 * (t + 1)] for t in range(TILES)]
        return jnp.concatenate(pieces + [label.astype(jnp.float32)], axis=0).astype(jnp.bfloat16)

    loads[0].wait()
    loads[1].wait()
    text_dir, text_norm = normalize(caption_ref[...].astype(jnp.float32))
    label = jnp.where(lane == 0, column(tclass_ref, row, 0, 15), jnp.where(lane == 1, blk, grp * ROWS + row))
    own_text[...] = block_of(text_dir, label)
    loads[2].wait()
    embedded = jnp.zeros((ROWS, D), jnp.float32)
    for n in range(CHUNKS):
        loads[3 + n].wait()
        at = slice(rows_w * n, rows_w * (n + 1))
        embedded += jnp.dot(pooled_ref[:, at], w_ref[at, :], preferred_element_type=jnp.float32)
    image_dir, image_norm = normalize(embedded)
    loads[-2].wait()
    loads[-1].wait()
    label = jnp.where(
        lane == 0, column(iclass_ref, row, 0, 15),
        jnp.where(lane == 1, column(slot_ref, row, 7, 63), column(slot_ref, row, 0, 127)),
    )
    img[0, 0, 0] = block_of(image_dir, label)

    pl.semaphore_wait(barrier, len(partners))

    started = []

    def copy(src, dst, **to):
        n = copy.count
        copy.count += 1
        c = pltpu.make_async_remote_copy(
            src_ref=src, dst_ref=dst, send_sem=send.at[n], recv_sem=recv.at[n],
            device_id=device(**to), device_id_type=MESH,
        )
        c.start()
        started.append(c)
        return c

    copy.count = 0

    def drain():
        while started:
            started.pop(0).wait_send()

    near = [copy(own_text, ztxt.at[0, i], dz=-b) for i, b in enumerate(TEXT_Z[0])]
    along = {}
    for p in (3, 2, 1, 0):
        for i in (1, 0):
            k = IMAGE_Z[p][i]
            if k:
                along[p, i] = copy(img.at[0, 0, 0], img.at[0, p, i], dz=-sign * k)

    plane_i = {}

    def forward_image(p):
        for i in (0, 1):
            if IMAGE_Z[p][i]:
                along[p, i].wait_recv()
        for q in (3, 2, 1):
            ax, ay = IMAGE_XY[q]
            plane_i[p, q] = copy(img.at[0, p], img.at[q, p], dx=-sign * ax, dy=-sign * ay)

    def forward_text(p):
        return [copy(ztxt.at[p], txt.at[p, 0, q], dx=-bx, dy=-by) for q, (bx, by) in enumerate(TEXT_XY)]

    def spread(pair, dst, label, n):
        a, b = pair[0].astype(jnp.float32), pair[1].astype(jnp.float32)
        at = slice(16 * n, 16 * n + 16)
        dst[at, :] = jnp.concatenate([unfold(a), unfold(b)], axis=0).astype(jnp.bfloat16)
        label[at, :] = jnp.concatenate([a[ROWS * TILES :], b[ROWS * TILES :]], axis=0).astype(jnp.bfloat16)

    def spread_image(p, q):
        if q:
            plane_i[p, q].wait_recv()
        spread(img.at[q, p], x_ref, mx_ref, 4 * q + p)

    def spread_text(p, h, q):
        spread(txt.at[p, h, q], y_ref, my_ref, 8 * p + 4 * h + q)

    forward_image(0)
    forward_image(1)
    forward_image(2)
    for c in near:
        c.wait_recv()
    middle = [copy(ztxt.at[0, i], via.at[i], dz=-b) for i, b in enumerate(TEXT_Z[0])]
    plane_t = forward_text(0)
    forward_image(3)
    for p in range(4):
        spread_image(p, 0)
    for p in range(3):
        for q in (1, 2, 3):
            spread_image(p, q)

    def cross_text(p, plane):
        across = []
        for q in range(4):
            plane[q].wait_recv()
            across.append(copy(txt.at[p, 0, q], txt.at[p, 1, q], other=True))
        return across

    across = cross_text(0, plane_t)
    for q in (1, 2, 3):
        spread_image(3, q)
    for c in middle:
        c.wait_recv()
    far = [copy(via.at[i], ztxt.at[1, i], dz=-b) for i, b in enumerate(TEXT_Z[0])]

    scale, offset = scale_ref[0], offset_ref[0]
    basis = jnp.where(
        row == 0, jnp.where(lane == 0, 1.0, 0.0),
        jnp.where(row == 1, jnp.where(lane == 1, 128.0, jnp.where(lane == 2, 1.0, 0.0)), 0.0),
    ).astype(jnp.bfloat16)
    image_columns = lax.dot_general(mx_ref[...], basis, NT, preferred_element_type=jnp.float32)

    def weigh(p):
        at = slice(128 * p, 128 * p + 128)
        scores = lax.dot_general(x_ref[...], y_ref[at, :], NT, preferred_element_type=jnp.float32) * scale + offset
        text_rows = lax.dot_general(basis, my_ref[at, :], NT, preferred_element_type=jnp.float32)
        positive = image_columns[:, 1:2] == text_rows[1:2, :]
        same = image_columns[:, 0:1] == text_rows[0:1, :]
        sigmoid = 1.0 / (1.0 + jnp.exp(jnp.where(positive, scores, -scores)))
        signed = jnp.where(positive, -scale, jnp.where(same, 0.0, scale))
        weight = (sigmoid * signed).astype(jnp.bfloat16)
        tg_ref[at, :] = lax.dot_general(weight, x_ref[...], TN, preferred_element_type=jnp.float32)
        for n in range(8):
            r0[p, n] = fold(tg_ref[128 * p + 64 + 8 * n : 128 * p + 72 + 8 * n, :])
        return weight, copy(r0.at[p], r0_in.at[p], other=True)

    def back_text(p, crossed):
        crossed.wait_recv()
        out = []
        for q, (bx, by) in enumerate(TEXT_XY):
            for i in (0, 1):
                n = 2 * q + i
                mine = tg_ref[128 * p + 8 * n : 128 * p + 8 * n + 8, :]
                rt1[p, q, i] = fold(mine + unfold(r0_in[p, n].astype(jnp.float32)))
            out.append(copy(rt1.at[p, q], rt1_in.at[p, q], dx=bx, dy=by))
        return out

    def home_text(p, arriving):
        for c in arriving:
            c.wait_recv()
        out = []
        for i, b in enumerate(TEXT_Z[p]):
            total = rt1_in[p, 0, i].astype(jnp.float32)
            for q in (1, 2, 3):
                total += rt1_in[p, q, i].astype(jnp.float32)
            rt2[p, i] = total.astype(jnp.bfloat16)
            out.append(copy(rt2.at[p, i], rt2_in.at[p, i], dz=b))
        return out

    for q in range(4):
        spread_text(0, 0, q)
    for q in range(4):
        across[q].wait_recv()
        spread_text(0, 1, q)
    weight, crossed = weigh(0)
    ig_ref[...] = jnp.dot(weight, y_ref[0:128, :], preferred_element_type=jnp.float32)
    returning = back_text(0, crossed)

    for c in far:
        c.wait_recv()
    plane_t = forward_text(1)
    home_t = home_text(0, returning)
    for n in range(FEATS // 128):
        at = slice(128 * n, 128 * n + 128)
        wt_ref[:, at] = w_ref[at, :].T
    across = cross_text(1, plane_t)
    for q in range(4):
        spread_text(1, 0, q)
    for q in range(4):
        across[q].wait_recv()
        spread_text(1, 1, q)
    weight, crossed = weigh(1)
    ig_ref[...] += jnp.dot(weight, y_ref[128:256, :], preferred_element_type=jnp.float32)
    back_i = {}
    for p in (3, 2, 1, 0):
        for q in (3, 2, 1, 0):
            ax, ay = IMAGE_XY[q]
            for i in (0, 1):
                n = 8 * q + 2 * p + i
                ri1[q, p, i] = fold(ig_ref[8 * n : 8 * n + 8, :])
            if q:
                back_i[p, q] = copy(ri1.at[q, p], ri1_in.at[q, p], dx=sign * ax, dy=sign * ay)
        if p == 3:
            returning = back_text(1, crossed)

    home_i = []

    def home_image(p):
        for q in (3, 2, 1):
            back_i[p, q].wait_recv()
        for i in (1, 0):
            total = ri1[0, p, i].astype(jnp.float32)
            for q in (1, 2, 3):
                total += ri1_in[q, p, i].astype(jnp.float32)
            ri2[p, i] = total.astype(jnp.bfloat16)
            if IMAGE_Z[p][i]:
                home_i.append(copy(ri2.at[p, i], ri2_in.at[p, i], dz=sign * IMAGE_Z[p][i]))

    home_image(3)
    home_t += home_text(1, returning)
    home_image(2)
    home_image(1)
    home_image(0)
    drain()

    for c in home_i:
        c.wait_recv()
    total = ri2[0, 0].astype(jnp.float32)
    for p in range(4):
        for i in (0, 1):
            if IMAGE_Z[p][i]:
                total += ri2_in[p, i].astype(jnp.float32)
    grad = unfold(total)
    inner = jnp.sum(image_dir * grad, axis=1, keepdims=True)
    embed_grad = ((grad - image_dir * inner) / image_norm).astype(jnp.bfloat16)
    image_out[...] = jnp.dot(embed_grad, wt_ref[...], preferred_element_type=jnp.float32).astype(jnp.bfloat16)
    for c in home_t:
        c.wait_recv()
    total = rt2_in[0, 0].astype(jnp.float32)
    for p, i in ((0, 1), (1, 0), (1, 1)):
        total += rt2_in[p, i].astype(jnp.float32)
    grad = unfold(total)
    inner = jnp.sum(text_dir * grad, axis=1, keepdims=True)
    text_out[...] = ((grad - text_dir * inner) / text_norm).astype(jnp.bfloat16)


def body(
    pooled_picture_vectors,
    picture_mapping_matrix,
    caption_vectors,
    matching_caption_slot,
    picture_instance_class,
    caption_instance_class,
    score_scale,
    score_offset,
):
    smem = pl.BlockSpec(memory_space=pltpu.SMEM)
    vmem = pl.BlockSpec(memory_space=pltpu.VMEM)
    hbm = pl.BlockSpec(memory_space=pltpu.HBM)
    half = jnp.bfloat16
    block = (FOLD, 128)
    return pl.pallas_call(
        kernel,
        out_shape=(
            jax.ShapeDtypeStruct((ROWS, FEATS), half),
            jax.ShapeDtypeStruct((ROWS, D), half),
        ),
        in_specs=[smem] * 2 + [hbm] * 6,
        out_specs=(vmem, vmem),
        scratch_shapes=[
            pltpu.SMEM((ROWS,), jnp.int32),
            pltpu.SMEM((ROWS,), jnp.int32),
            pltpu.SMEM((ROWS,), jnp.int32),
            pltpu.VMEM((ROWS, FEATS), half),
            pltpu.VMEM((ROWS, D), half),
            pltpu.VMEM((FEATS, D), half),
            pltpu.VMEM((D, FEATS), half),
            pltpu.VMEM(block, half),
            pltpu.VMEM((4, 4, 2) + block, half),
            pltpu.VMEM((2, 2) + block, half),
            pltpu.VMEM((2,) + block, half),
            pltpu.VMEM((2, 2, 4, 2) + block, half),
            pltpu.VMEM((256, D), half),
            pltpu.VMEM((256, D), half),
            pltpu.VMEM((256, 128), half),
            pltpu.VMEM((256, 128), half),
            pltpu.VMEM((256, D), jnp.float32),
            pltpu.VMEM((256, D), jnp.float32),
            pltpu.VMEM((2, 8) + block, half),
            pltpu.VMEM((2, 8) + block, half),
            pltpu.VMEM((2, 4, 2) + block, half),
            pltpu.VMEM((2, 4, 2) + block, half),
            pltpu.VMEM((2, 2) + block, half),
            pltpu.VMEM((2, 2) + block, half),
            pltpu.VMEM((4, 4, 2) + block, half),
            pltpu.VMEM((4, 4, 2) + block, half),
            pltpu.VMEM((4, 2) + block, half),
            pltpu.VMEM((4, 2) + block, half),
            pltpu.SemaphoreType.DMA((8,)),
            pltpu.SemaphoreType.DMA((80,)),
            pltpu.SemaphoreType.DMA((80,)),
        ],
        compiler_params=pltpu.CompilerParams(
            collective_id=0, has_side_effects=True, vmem_limit_bytes=60 * 2**20
        ),
        name="contrast",
    )(
        score_scale, score_offset, matching_caption_slot, picture_instance_class, caption_instance_class,
        pooled_picture_vectors, caption_vectors, picture_mapping_matrix,
    )


def solution(mesh):
    placed = (
        P(("blk", "grp"), None),
        P(),
        P(("blk", "grp"), None),
        P(("blk", "grp")),
        P(("blk", "grp")),
        P(("blk", "grp")),
        P(),
        P(),
    )
    return jax.shard_map(
        body,
        mesh=mesh,
        in_specs=placed,
        out_specs=(P(("blk", "grp"), None), P(("blk", "grp"), None)),
        check_vma=False,
    )
```

time: 87.2 us -> 74.1 us (0.85)
  the two profiles are of different devices: /device:TPU:25 before, /device:TPU:8 now
where the time goes in v2:
time: 74.1 us; the launch traced here: 73.8 us
  Pallas kernels  69.2 us (93%)
  local copies, waits for them, and re-layouts  2.68 us (4%)
  between operations  1.93 us (3%)
    pallas_call x1, Pallas kernels, body(): pl.pallas_call(kernel, out_shape=(jax.ShapeDtypeStruct((ROWS, FEATS), hal...  69.2 us
    unnamed x2, local copies, waits for them, and re-layouts  2.68 us

profile of v2, /device:TPU:8, one launch (start us, length us, event | category | flops | bytes accessed | tf_op | source)
XLA Modules:
  0.0 73.8 jit_solution(298507027333039483)
XLA Ops:
  1.9 69.2 %contrast.1 = (bf16[8,1536]{1,0:T(8,128)(2,1)}, bf16[8,1152]{1,0:T(8,128)(2,1)}) custom-call(f32[1]{0:T(128)S(6)} %copy.12.scale_ref, f32[1]{0:T(128)S(6)} %copy.13.offset_ref, s32[8]{0:T(128)} %slot_hbm.1, s32[8]{0:T(128)} %iclass_hbm.1, s32[8]{0:T(128)} %tclass_hbm.1, bf16[8,1536]{1,0:T(8,128)(2,1)} %pooled_hbm.1, bf16[8,1152]{1,0:T(8,128)(2,1)} %caption_hbm.1, ...), custom_call_target="tpu_custom_call" | custom-call | tf_op jit(solution)/shard_map/contrast/pallas_call | solution.py:330
  71.2 1.3 %copy.14 = bf16[8,1536]{1,0:T(8,128)(2,1)} copy(bf16[8,1536]{1,0:T(8,128)(2,1)} %get-tuple-element.4) | data formatting | bytes 49152
  72.5 1.3 %copy.15 = bf16[8,1152]{1,0:T(8,128)(2,1)} copy(bf16[8,1152]{1,0:T(8,128)(2,1)} %get-tuple-element.5) | data formatting | bytes 36864

commit v3 on v2

v3 whole, which is shorter than its diff:
```python
import jax
import jax.numpy as jnp
from jax import lax
from jax.experimental import pallas as pl
from jax.experimental.pallas import tpu as pltpu
from jax.sharding import PartitionSpec as P

epsilon = 1e-06
D = 1152
FEATS = 1536
ROWS = 8
TILES = D // 128
FOLD = (TILES + 1) * ROWS
MESH = pl.DeviceIdType.MESH

IMAGE_Z = ((0, -1), (1, -2), (2, -3), (3, -4))
TEXT_Z = (-4, 4, -12, 12)
IMAGE_XY = ((0, 0), (1, 0), (0, 1), (1, 1))
TEXT_XY = ((1, 1), (1, -1), (-1, 1), (-1, -1))
CHUNKS = 3
NT = (((1,), (1,)), ((), ()))
TN = (((0,), (0,)), ((), ()))


def fold(rows):
    pieces = [rows[:, 128 * t : 128 * (t + 1)] for t in range(TILES)]
    pieces.append(jnp.zeros((ROWS, 128), jnp.float32))
    return jnp.concatenate(pieces, axis=0).astype(jnp.bfloat16)


def unfold(block):
    return jnp.concatenate([block[ROWS * t : ROWS * (t + 1)] for t in range(TILES)], axis=1)


def normalize(values):
    norm_rows = jnp.sqrt(jnp.sum(values * values, axis=1, keepdims=True) + epsilon)
    return values / norm_rows, norm_rows


def column(ref, row, shift, mask):
    out = jnp.zeros((ROWS, 128), jnp.int32)
    for r in range(ROWS):
        out = jnp.where(row == r, lax.bitwise_and(lax.shift_right_logical(ref[r], shift), mask), out)
    return out


def kernel(
    scale_hbm, offset_hbm, slot_hbm, iclass_hbm, tclass_hbm, pooled_hbm, caption_hbm, w_hbm,
    image_out, text_out,
    scale_ref, offset_ref, slot_ref, iclass_ref, tclass_ref, pooled_ref, caption_ref, w_ref, wt_ref,
    own_text, img, img_s, ztxt, txt, txt_s, x_ref, mx_ref, y_ref, my_ref, tg_ref, ig_ref,
    rt1, rt1_in, rt2, rt2_in, ri1, ri1_in, ri2, ri2_in,
    load, send, recv,
):
    blk = lax.axis_index("blk")
    grp = lax.axis_index("grp")
    x, y, z, core = (blk // 4) % 4, blk % 4, (blk // 16) * 8 + grp // 2, grp % 2
    sign = 1 - 2 * core

    def device(dx=0, dy=0, dz=0, other=False):
        to_x, to_y, to_z = (x + dx + 4) % 4, (y + dy + 4) % 4, (z + dz + 32) % 32
        to_core = 1 - core if other else core
        return ((to_z // 8) * 16 + to_x * 4 + to_y, (to_z % 8) * 2 + to_core)

    partners = [dict(dz=d) for d in (-4, 4, -3, 3, -2, 2, -1, 1)]
    partners += [dict(dx=dx, dy=dy) for dx in (-1, 0, 1) for dy in (-1, 0, 1) if dx or dy]
    partners += [dict(other=True)]
    barrier = pltpu.get_barrier_semaphore()

    def greet(some):
        for p in some:
            pl.semaphore_signal(barrier, inc=1, device_id=device(**p), device_id_type=MESH)

    rows_w = FEATS // CHUNKS
    loads = [
        pltpu.make_async_copy(src, dst, load.at[n])
        for n, (src, dst) in enumerate(
            [(caption_hbm, caption_ref), (tclass_hbm, tclass_ref), (pooled_hbm, pooled_ref)]
            + [(w_hbm.at[pl.ds(rows_w * n, rows_w)], w_ref.at[pl.ds(rows_w * n, rows_w)]) for n in range(CHUNKS)]
            + [(iclass_hbm, iclass_ref), (slot_hbm, slot_ref), (scale_hbm, scale_ref), (offset_hbm, offset_ref)]
        )
    ]
    greet(partners[:4])
    for c in loads:
        c.start()
    greet(partners[4:])

    row = lax.broadcasted_iota(jnp.int32, (ROWS, 128), 0)
    lane = lax.broadcasted_iota(jnp.int32, (ROWS, 128), 1)

    def block_of(values, label):
        pieces = [values[:, 128 * t : 128 * (t + 1)] for t in range(TILES)]
        return jnp.concatenate(pieces + [label.astype(jnp.float32)], axis=0).astype(jnp.bfloat16)

    started = []

    def copy(src, dst, **to):
        n = copy.count
        copy.count += 1
        c = pltpu.make_async_remote_copy(
            src_ref=src, dst_ref=dst, send_sem=send.at[n], recv_sem=recv.at[n],
            device_id=device(**to), device_id_type=MESH,
        )
        c.start()
        started.append(c)
        return c

    copy.count = 0

    def arrive(copies):
        for c in copies:
            c.wait_recv()

    def drain():
        while started:
            started.pop(0).wait_send()

    loads[0].wait()
    loads[1].wait()
    text_dir, text_norm = normalize(caption_ref[...].astype(jnp.float32))
    label = jnp.where(lane == 0, column(tclass_ref, row, 0, 15), jnp.where(lane == 1, blk, grp * ROWS + row))
    own_text[...] = block_of(text_dir, label)
    pl.semaphore_wait(barrier, len(partners))
    near = [copy(own_text, ztxt.at[u], dz=-TEXT_Z[u]) for u in (0, 1)]

    loads[2].wait()
    embedded = jnp.zeros((ROWS, D), jnp.float32)
    for n in range(CHUNKS):
        loads[3 + n].wait()
        at = slice(rows_w * n, rows_w * (n + 1))
        embedded += jnp.dot(pooled_ref[:, at], w_ref[at, :], preferred_element_type=jnp.float32)
    image_dir, image_norm = normalize(embedded)
    for c in loads[3 + CHUNKS :]:
        c.wait()
    label = jnp.where(
        lane == 0, column(iclass_ref, row, 0, 15),
        jnp.where(lane == 1, column(slot_ref, row, 7, 63), column(slot_ref, row, 0, 127)),
    )
    img[0, 0, 0] = block_of(image_dir, label)
    along = {}
    for p in (3, 2, 1, 0):
        for i in (1, 0):
            k = IMAGE_Z[p][i]
            if k:
                along[p, i] = copy(img.at[0, 0, 0], img.at[p, 0, i], dz=-sign * k)

    def plane_text(u):
        return [copy(ztxt.at[u], txt.at[u, q], dx=-bx, dy=-by) for q, (bx, by) in enumerate(TEXT_XY)]

    plane_i, plane_t = {}, {}

    def plane_image(p):
        for i in (0, 1):
            if IMAGE_Z[p][i]:
                along[p, i].wait_recv()
        for q in (3, 2, 1):
            ax, ay = IMAGE_XY[q]
            plane_i[p, q] = copy(img.at[p, 0], img.at[p, q], dx=-sign * ax, dy=-sign * ay)

    arrive(near)
    far = [copy(ztxt.at[u], ztxt.at[2 + u], dz=-2 * TEXT_Z[u]) for u in (0, 1)]
    plane_t[0] = plane_text(0)
    plane_t[1] = plane_text(1)
    for p in range(4):
        plane_image(p)

    def spread(pair, dst, label, at):
        a, b = pair[0].astype(jnp.float32), pair[1].astype(jnp.float32)
        at = slice(at, at + 16)
        dst[at, :] = jnp.concatenate([unfold(a), unfold(b)], axis=0).astype(jnp.bfloat16)
        label[at, :] = jnp.concatenate([a[ROWS * TILES :], b[ROWS * TILES :]], axis=0).astype(jnp.bfloat16)

    cross_i, cross_t = {}, {}

    def take_image(p):
        for q in (1, 2, 3):
            plane_i[p, q].wait_recv()
        cross_i[p] = copy(img.at[p], img_s.at[p], other=True)
        for q in range(4):
            spread(img.at[p, q], x_ref, mx_ref, 64 * p + 16 * q)

    def take_text(u):
        arrive(plane_t[u])
        cross_t[u] = copy(txt.at[u], txt_s.at[u], other=True)
        for m in (0, 1):
            spread(txt.at[u, pl.ds(2 * m, 2)], y_ref, my_ref, 32 * u + 16 * m)

    def take_text_cross(u):
        cross_t[u].wait_recv()
        for m in (0, 1):
            spread(txt_s.at[u, pl.ds(2 * m, 2)], y_ref, my_ref, 128 + 32 * u + 16 * m)

    take_image(0)
    take_image(1)
    for u in (2, 3):
        far[u - 2].wait_recv()
        plane_t[u] = plane_text(u)
    take_text(0)
    take_text(1)
    take_image(2)
    take_image(3)
    take_text(2)
    take_text(3)

    scale, offset = scale_ref[0], offset_ref[0]
    basis = jnp.where(
        row == 0, jnp.where(lane == 0, 1.0, 0.0),
        jnp.where(row == 1, jnp.where(lane == 1, 128.0, jnp.where(lane == 2, 1.0, 0.0)), 0.0),
    ).astype(jnp.bfloat16)
    def weights(texts, images):
        scores = lax.dot_general(y_ref[texts, :], x_ref[images, :], NT, preferred_element_type=jnp.float32)
        scores = scores * scale + offset
        text_columns = lax.dot_general(my_ref[texts, :], basis, NT, preferred_element_type=jnp.float32)
        image_rows = lax.dot_general(basis, mx_ref[images, :], NT, preferred_element_type=jnp.float32)
        positive = text_columns[:, 1:2] == image_rows[1:2, :]
        same = text_columns[:, 0:1] == image_rows[0:1, :]
        sigmoid = 1.0 / (1.0 + jnp.exp(jnp.where(positive, scores, -scores)))
        signed = jnp.where(positive, -scale, jnp.where(same, 0.0, scale))
        return (sigmoid * signed).astype(jnp.bfloat16)

    def home_text(u):
        arrive(back_t[u])
        total = rt1_in[u, 0].astype(jnp.float32)
        for q in (1, 2, 3):
            total += rt1_in[u, q].astype(jnp.float32)
        rt2[u] = total.astype(jnp.bfloat16)
        return copy(rt2.at[u], rt2_in.at[u], dz=TEXT_Z[u])

    back_t, home_t = {}, {}
    own, other = slice(0, 128), slice(128, 256)
    weight = weights(own, slice(0, 256))
    tg_ref[...] = jnp.dot(weight, x_ref[0:256, :], preferred_element_type=jnp.float32)
    ig_ref[...] = lax.dot_general(weight, y_ref[own, :], TN, preferred_element_type=jnp.float32)
    for p in range(4):
        cross_i[p].wait_recv()
        for q in range(4):
            spread(img_s.at[p, q], x_ref, mx_ref, 256 + 64 * p + 16 * q)
    weight = weights(own, slice(256, 512))
    tg_ref[...] += jnp.dot(weight, x_ref[256:512, :], preferred_element_type=jnp.float32)
    for u in (2, 3, 0, 1):
        back_t[u] = []
        for q, (bx, by) in enumerate(TEXT_XY):
            n = 32 * u + 8 * q
            rt1[u, q] = fold(tg_ref[n : n + 8, :])
            back_t[u].append(copy(rt1.at[u, q], rt1_in.at[u, q], dx=bx, dy=by))
    for u in range(4):
        take_text_cross(u)
    weight = weights(other, slice(0, 256))
    ig_ref[...] += lax.dot_general(weight, y_ref[other, :], TN, preferred_element_type=jnp.float32)
    back_i = {}
    for p in (3, 2, 1, 0):
        for q in (3, 2, 1, 0):
            ax, ay = IMAGE_XY[q]
            for i in (0, 1):
                n = 64 * p + 16 * q + 8 * i
                ri1[p, q, i] = fold(ig_ref[n : n + 8, :])
            if q:
                back_i[p, q] = copy(ri1.at[p, q], ri1_in.at[p, q], dx=sign * ax, dy=sign * ay)

    home_i = []

    def home_image(p):
        for q in (3, 2, 1):
            back_i[p, q].wait_recv()
        for i in (1, 0):
            total = ri1[p, 0, i].astype(jnp.float32)
            for q in (1, 2, 3):
                total += ri1_in[p, q, i].astype(jnp.float32)
            ri2[p, i] = total.astype(jnp.bfloat16)
            if IMAGE_Z[p][i]:
                home_i.append(copy(ri2.at[p, i], ri2_in.at[p, i], dz=sign * IMAGE_Z[p][i]))

    home_t[2] = home_text(2)
    home_t[3] = home_text(3)
    for n in range(FEATS // 128):
        at = slice(128 * n, 128 * n + 128)
        wt_ref[:, at] = w_ref[at, :].T
    for p in (3, 2, 1, 0):
        home_image(p)
    home_t[0] = home_text(0)
    home_t[1] = home_text(1)
    drain()

    arrive(home_i)
    total = ri2[0, 0].astype(jnp.float32)
    for p in range(4):
        for i in (0, 1):
            if IMAGE_Z[p][i]:
                total += ri2_in[p, i].astype(jnp.float32)
    grad = unfold(total)
    inner = jnp.sum(image_dir * grad, axis=1, keepdims=True)
    embed_grad = ((grad - image_dir * inner) / image_norm).astype(jnp.bfloat16)
    image_out[...] = jnp.dot(embed_grad, wt_ref[...], preferred_element_type=jnp.float32).astype(jnp.bfloat16)
    arrive([home_t[u] for u in range(4)])
    total = rt2_in[0].astype(jnp.float32)
    for u in (1, 2, 3):
        total += rt2_in[u].astype(jnp.float32)
    grad = unfold(total)
    inner = jnp.sum(text_dir * grad, axis=1, keepdims=True)
    text_out[...] = ((grad - text_dir * inner) / text_norm).astype(jnp.bfloat16)


def body(
    pooled_picture_vectors,
    picture_mapping_matrix,
    caption_vectors,
    matching_caption_slot,
    picture_instance_class,
    caption_instance_class,
    score_scale,
    score_offset,
):
    vmem = pl.BlockSpec(memory_space=pltpu.VMEM)
    hbm = pl.BlockSpec(memory_space=pltpu.HBM)
    half = jnp.bfloat16
    block = (FOLD, 128)
    return pl.pallas_call(
        kernel,
        out_shape=(
            pltpu.VMEM((ROWS, FEATS), half),
            pltpu.VMEM((ROWS, D), half),
        ),
        in_specs=[hbm] * 8,
        out_specs=(vmem, vmem),
        scratch_shapes=[
            pltpu.SMEM((1,), jnp.float32),
            pltpu.SMEM((1,), jnp.float32),
            pltpu.SMEM((ROWS,), jnp.int32),
            pltpu.SMEM((ROWS,), jnp.int32),
            pltpu.SMEM((ROWS,), jnp.int32),
            pltpu.VMEM((ROWS, FEATS), half),
            pltpu.VMEM((ROWS, D), half),
            pltpu.VMEM((FEATS, D), half),
            pltpu.VMEM((D, FEATS), half),
            pltpu.VMEM(block, half),
            pltpu.VMEM((4, 4, 2) + block, half),
            pltpu.VMEM((4, 4, 2) + block, half),
            pltpu.VMEM((4,) + block, half),
            pltpu.VMEM((4, 4) + block, half),
            pltpu.VMEM((4, 4) + block, half),
            pltpu.VMEM((512, D), half),
            pltpu.VMEM((512, 128), half),
            pltpu.VMEM((256, D), half),
            pltpu.VMEM((256, 128), half),
            pltpu.VMEM((128, D), jnp.float32),
            pltpu.VMEM((256, D), jnp.float32),
            pltpu.VMEM((4, 4) + block, half),
            pltpu.VMEM((4, 4) + block, half),
            pltpu.VMEM((4,) + block, half),
            pltpu.VMEM((4,) + block, half),
            pltpu.VMEM((4, 4, 2) + block, half),
            pltpu.VMEM((4, 4, 2) + block, half),
            pltpu.VMEM((4, 2) + block, half),
            pltpu.VMEM((4, 2) + block, half),
            pltpu.SemaphoreType.DMA((10,)),
            pltpu.SemaphoreType.DMA((96,)),
            pltpu.SemaphoreType.DMA((96,)),
        ],
        compiler_params=pltpu.CompilerParams(
            collective_id=0, has_side_effects=True, vmem_limit_bytes=60 * 2**20
        ),
        name="contrast",
    )(
        score_scale, score_offset, matching_caption_slot, picture_instance_class, caption_instance_class,
        pooled_picture_vectors, caption_vectors, picture_mapping_matrix,
    )


def solution(mesh):
    placed = (
        P(("blk", "grp"), None),
        P(),
        P(("blk", "grp"), None),
        P(("blk", "grp")),
        P(("blk", "grp")),
        P(("blk", "grp")),
        P(),
        P(),
    )
    return jax.shard_map(
        body,
        mesh=mesh,
        in_specs=placed,
        out_specs=(P(("blk", "grp"), None), P(("blk", "grp"), None)),
        check_vma=False,
    )
```

time: 74.1 us -> 66 us (0.89)
  the two profiles are of different devices: /device:TPU:8 before, /device:TPU:1 now
where the time goes in v3:
time: 66 us; the launch traced here: 65.9 us
  Pallas kernels  62.7 us (95%)
  between operations  1.93 us (3%)
  local copies, waits for them, and re-layouts  1.22 us (2%)
    pallas_call x1, Pallas kernels, body(): pl.pallas_call(kernel, out_shape=(pltpu.VMEM((ROWS, FEATS), half), pltpu....  62.7 us

profile of v3, /device:TPU:1, one launch (start us, length us, event | category | flops | bytes accessed | tf_op | source)
XLA Modules:
  0.0 65.9 jit_solution(3222403273329762040)
XLA Ops:
  1.9 62.7 %contrast.1 = (bf16[8,1536]{1,0:T(8,128)(2,1)S(1)}, bf16[8,1152]{1,0:T(8,128)(2,1)S(1)}) custom-call(f32[1]{0:T(128)S(6)} %copy.14.scale_hbm, f32[1]{0:T(128)S(6)} %copy.15.offset_hbm, s32[8]{0:T(128)} %slot_hbm.1, s32[8]{0:T(128)} %iclass_hbm.1, s32[8]{0:T(128)} %tclass_hbm.1, bf16[8,1536]{1,0:T(8,128)(2,1)} %pooled_hbm.1, bf16[8,1152]{1,0:T(8,128)(2,1)} %caption_hbm.1, ...), custom_call_target="tpu_custom_call" | custom-call | tf_op jit(solution)/shard_map/contrast/pallas_call | solution.py:317
  64.6 0.6 copy.12
  65.2 0.6 copy.13

commit v4 on v3

--- a/solution.py
+++ b/solution.py
@@ -56,6 +56,7 @@
     grp = lax.axis_index("grp")
     x, y, z, core = (blk // 4) % 4, blk % 4, (blk // 16) * 8 + grp // 2, grp % 2
     sign = 1 - 2 * core
+    turn = -sign
 
     def device(dx=0, dy=0, dz=0, other=False):
         to_x, to_y, to_z = (x + dx + 4) % 4, (y + dy + 4) % 4, (z + dz + 32) % 32
@@ -94,9 +95,10 @@
 
     started = []
 
-    def copy(src, dst, **to):
-        n = copy.count
-        copy.count += 1
+    def copy(src, dst, n=None, **to):
+        if n is None:
+            n = copy.count
+            copy.count += 1
         c = pltpu.make_async_remote_copy(
             src_ref=src, dst_ref=dst, send_sem=send.at[n], recv_sem=recv.at[n],
             device_id=device(**to), device_id_type=MESH,
@@ -155,7 +157,7 @@
                 along[p, i].wait_recv()
         for q in (3, 2, 1):
             ax, ay = IMAGE_XY[q]
-            plane_i[p, q] = copy(img.at[p, 0], img.at[p, q], dx=-sign * ax, dy=-sign * ay)
+            plane_i[p, q] = copy(img.at[p, 0], img.at[p, q], dx=-turn * ax, dy=-turn * ay)
 
     arrive(near)
     far = [copy(ztxt.at[u], ztxt.at[2 + u], dz=-2 * TEXT_Z[u]) for u in (0, 1)]
@@ -218,15 +220,26 @@
         signed = jnp.where(positive, -scale, jnp.where(same, 0.0, scale))
         return (sigmoid * signed).astype(jnp.bfloat16)
 
-    def home_text(u):
-        arrive(back_t[u])
+    far_first = ((z + 4) // 16) % 2
+    ahead, behind = 2 * far_first, 2 - 2 * far_first
+
+    def plane_back(u):
+        out = []
+        for q, (bx, by) in enumerate(TEXT_XY):
+            n = pl.multiple_of(32 * u + 8 * q, 8)
+            rt1[u, q] = fold(tg_ref[pl.ds(n, 8), :])
+            out.append(copy(rt1.at[u, q], rt1_in.at[u, q], n=80 + 4 * u + q, dx=bx, dy=by))
+        return out
+
+    def home_text(u, arriving):
+        arrive(arriving)
         total = rt1_in[u, 0].astype(jnp.float32)
         for q in (1, 2, 3):
             total += rt1_in[u, q].astype(jnp.float32)
         rt2[u] = total.astype(jnp.bfloat16)
-        return copy(rt2.at[u], rt2_in.at[u], dz=TEXT_Z[u])
-
-    back_t, home_t = {}, {}
+        return copy(rt2.at[u], rt2_in.at[u], n=96 + u, dz=(2 * (u % 2) - 1) * (4 + 8 * (u // 2)))
+
+    home_t = []
     own, other = slice(0, 128), slice(128, 256)
     weight = weights(own, slice(0, 256))
     tg_ref[...] = jnp.dot(weight, x_ref[0:256, :], preferred_element_type=jnp.float32)
@@ -237,12 +250,7 @@
             spread(img_s.at[p, q], x_ref, mx_ref, 256 + 64 * p + 16 * q)
     weight = weights(own, slice(256, 512))
     tg_ref[...] += jnp.dot(weight, x_ref[256:512, :], preferred_element_type=jnp.float32)
-    for u in (2, 3, 0, 1):
-        back_t[u] = []
-        for q, (bx, by) in enumerate(TEXT_XY):
-            n = 32 * u + 8 * q
-            rt1[u, q] = fold(tg_ref[n : n + 8, :])
-            back_t[u].append(copy(rt1.at[u, q], rt1_in.at[u, q], dx=bx, dy=by))
+    back_ahead = [plane_back(ahead + i) for i in (0, 1)]
     for u in range(4):
         take_text_cross(u)
     weight = weights(other, slice(0, 256))
@@ -251,34 +259,35 @@
     for p in (3, 2, 1, 0):
         for q in (3, 2, 1, 0):
             ax, ay = IMAGE_XY[q]
-            for i in (0, 1):
-                n = 64 * p + 16 * q + 8 * i
-                ri1[p, q, i] = fold(ig_ref[n : n + 8, :])
+            n = 64 * p + 16 * q
+            pieces = [ig_ref[n : n + 16, 128 * t : 128 * (t + 1)] for t in range(TILES)]
+            ri1[p, q] = jnp.concatenate(pieces, axis=0).astype(jnp.bfloat16)
             if q:
-                back_i[p, q] = copy(ri1.at[p, q], ri1_in.at[p, q], dx=sign * ax, dy=sign * ay)
-
+                back_i[p, q] = copy(ri1.at[p, q], ri1_in.at[p, q], dx=turn * ax, dy=turn * ay)
+
+    back_behind = [plane_back(behind + i) for i in (0, 1)]
     home_i = []
 
     def home_image(p):
         for q in (3, 2, 1):
             back_i[p, q].wait_recv()
+        total = ri1[p, 0].astype(jnp.float32)
+        for q in (1, 2, 3):
+            total += ri1_in[p, q].astype(jnp.float32)
         for i in (1, 0):
-            total = ri1[p, 0, i].astype(jnp.float32)
-            for q in (1, 2, 3):
-                total += ri1_in[p, q, i].astype(jnp.float32)
-            ri2[p, i] = total.astype(jnp.bfloat16)
+            pieces = [total[16 * t + 8 * i : 16 * t + 8 * i + 8] for t in range(TILES)]
+            pieces.append(jnp.zeros((ROWS, 128), jnp.float32))
+            ri2[p, i] = jnp.concatenate(pieces, axis=0).astype(jnp.bfloat16)
             if IMAGE_Z[p][i]:
                 home_i.append(copy(ri2.at[p, i], ri2_in.at[p, i], dz=sign * IMAGE_Z[p][i]))
 
-    home_t[2] = home_text(2)
-    home_t[3] = home_text(3)
+    home_t += [home_text(ahead + i, back_ahead[i]) for i in (0, 1)]
     for n in range(FEATS // 128):
         at = slice(128 * n, 128 * n + 128)
         wt_ref[:, at] = w_ref[at, :].T
     for p in (3, 2, 1, 0):
         home_image(p)
-    home_t[0] = home_text(0)
-    home_t[1] = home_text(1)
+    home_t += [home_text(behind + i, back_behind[i]) for i in (0, 1)]
     drain()
 
     arrive(home_i)
@@ -291,7 +300,7 @@
     inner = jnp.sum(image_dir * grad, axis=1, keepdims=True)
     embed_grad = ((grad - image_dir * inner) / image_norm).astype(jnp.bfloat16)
     image_out[...] = jnp.dot(embed_grad, wt_ref[...], preferred_element_type=jnp.float32).astype(jnp.bfloat16)
-    arrive([home_t[u] for u in range(4)])
+    arrive(home_t)
     total = rt2_in[0].astype(jnp.float32)
     for u in (1, 2, 3):
         total += rt2_in[u].astype(jnp.float32)
@@ -348,13 +357,13 @@
             pltpu.VMEM((4, 4) + block, half),
             pltpu.VMEM((4,) + block, half),
             pltpu.VMEM((4,) + block, half),
-            pltpu.VMEM((4, 4, 2) + block, half),
-            pltpu.VMEM((4, 4, 2) + block, half),
+            pltpu.VMEM((4, 4, 2 * D // 16, 128), half),
+            pltpu.VMEM((4, 4, 2 * D // 16, 128), half),
             pltpu.VMEM((4, 2) + block, half),
             pltpu.VMEM((4, 2) + block, half),
             pltpu.SemaphoreType.DMA((10,)),
-            pltpu.SemaphoreType.DMA((96,)),
-            pltpu.SemaphoreType.DMA((96,)),
+            pltpu.SemaphoreType.DMA((100,)),
+            pltpu.SemaphoreType.DMA((100,)),
         ],
         compiler_params=pltpu.CompilerParams(
             collective_id=0, has_side_effects=True, vmem_limit_bytes=60 * 2**20

time: 66 us -> 64.8 us (0.982)
  the two profiles are of different devices: /device:TPU:1 before, /device:TPU:8 now
where the time goes in v4:
time: 64.8 us; the launch traced here: 64.7 us
  Pallas kernels  61.5 us (95%)
  between operations  1.93 us (3%)
  local copies, waits for them, and re-layouts  1.22 us (2%)
    pallas_call x1, Pallas kernels, body(): pl.pallas_call(kernel, out_shape=(pltpu.VMEM((ROWS, FEATS), half), pltpu....  61.5 us

profile of v4, /device:TPU:8, one launch (start us, length us, event | category | flops | bytes accessed | tf_op | source)
XLA Modules:
  0.0 64.7 jit_solution(3435516488882214026)
XLA Ops:
  1.9 61.5 %contrast.1 = (bf16[8,1536]{1,0:T(8,128)(2,1)S(1)}, bf16[8,1152]{1,0:T(8,128)(2,1)S(1)}) custom-call(f32[1]{0:T(128)S(6)} %copy.14.scale_hbm, f32[1]{0:T(128)S(6)} %copy.15.offset_hbm, s32[8]{0:T(128)} %slot_hbm.1, s32[8]{0:T(128)} %iclass_hbm.1, s32[8]{0:T(128)} %tclass_hbm.1, bf16[8,1536]{1,0:T(8,128)(2,1)} %pooled_hbm.1, bf16[8,1152]{1,0:T(8,128)(2,1)} %caption_hbm.1, ...), custom_call_target="tpu_custom_call" | custom-call | tf_op jit(solution)/shard_map/contrast/pallas_call | solution.py:326
  63.5 0.6 copy.12
  64.1 0.6 copy.13

commit v5 on v4

--- a/solution.py
+++ b/solution.py
@@ -16,7 +16,7 @@
 IMAGE_Z = ((0, -1), (1, -2), (2, -3), (3, -4))
 TEXT_Z = (-4, 4, -12, 12)
 IMAGE_XY = ((0, 0), (1, 0), (0, 1), (1, 1))
-TEXT_XY = ((1, 1), (1, -1), (-1, 1), (-1, -1))
+TEXT_XY = ((1, 1), (-1, -1), (1, -1), (-1, 1))
 CHUNKS = 3
 NT = (((1,), (1,)), ((), ()))
 TN = (((0,), (0,)), ((), ()))
@@ -147,7 +147,7 @@
                 along[p, i] = copy(img.at[0, 0, 0], img.at[p, 0, i], dz=-sign * k)
 
     def plane_text(u):
-        return [copy(ztxt.at[u], txt.at[u, q], dx=-bx, dy=-by) for q, (bx, by) in enumerate(TEXT_XY)]
+        return [copy(ztxt.at[u], txt.at[u, q], dx=-turn * bx, dy=-turn * by) for q, (bx, by) in enumerate(TEXT_XY)]
 
     plane_i, plane_t = {}, {}
 
@@ -220,24 +220,35 @@
         signed = jnp.where(positive, -scale, jnp.where(same, 0.0, scale))
         return (sigmoid * signed).astype(jnp.bfloat16)
 
-    far_first = ((z + 4) // 16) % 2
-    ahead, behind = 2 * far_first, 2 - 2 * far_first
-
-    def plane_back(u):
+    ahead = ((z + 4) // 16) % 2
+    behind = 1 - ahead
+
+    def plane_back(pair):
         out = []
         for q, (bx, by) in enumerate(TEXT_XY):
-            n = pl.multiple_of(32 * u + 8 * q, 8)
-            rt1[u, q] = fold(tg_ref[pl.ds(n, 8), :])
-            out.append(copy(rt1.at[u, q], rt1_in.at[u, q], n=80 + 4 * u + q, dx=bx, dy=by))
+            n = 64 * pair + 8 * q
+            both = [tg_ref[pl.ds(pl.multiple_of(n + 32 * i, 8), 8), :] for i in (0, 1)]
+            rows = jnp.concatenate(both, axis=0)
+            pieces = [rows[:, 128 * t : 128 * (t + 1)] for t in range(TILES)]
+            rt1[pair, q] = jnp.concatenate(pieces, axis=0).astype(jnp.bfloat16)
+            out.append(
+                copy(rt1.at[pair, q], rt1_in.at[pair, q], n=80 + 4 * pair + q, dx=turn * bx, dy=turn * by)
+            )
         return out
 
-    def home_text(u, arriving):
+    def home_text(pair, arriving):
         arrive(arriving)
-        total = rt1_in[u, 0].astype(jnp.float32)
+        total = rt1_in[pair, 0].astype(jnp.float32)
         for q in (1, 2, 3):
-            total += rt1_in[u, q].astype(jnp.float32)
-        rt2[u] = total.astype(jnp.bfloat16)
-        return copy(rt2.at[u], rt2_in.at[u], n=96 + u, dz=(2 * (u % 2) - 1) * (4 + 8 * (u // 2)))
+            total += rt1_in[pair, q].astype(jnp.float32)
+        out = []
+        for i in (0, 1):
+            u = 2 * pair + i
+            pieces = [total[16 * t + 8 * i : 16 * t + 8 * i + 8] for t in range(TILES)]
+            pieces.append(jnp.zeros((ROWS, 128), jnp.float32))
+            rt2[u] = jnp.concatenate(pieces, axis=0).astype(jnp.bfloat16)
+            out.append(copy(rt2.at[u], rt2_in.at[u], n=96 + u, dz=(2 * i - 1) * (4 + 8 * pair)))
+        return out
 
     home_t = []
     own, other = slice(0, 128), slice(128, 256)
@@ -250,7 +261,7 @@
             spread(img_s.at[p, q], x_ref, mx_ref, 256 + 64 * p + 16 * q)
     weight = weights(own, slice(256, 512))
     tg_ref[...] += jnp.dot(weight, x_ref[256:512, :], preferred_element_type=jnp.float32)
-    back_ahead = [plane_back(ahead + i) for i in (0, 1)]
+    back_ahead = plane_back(ahead)
     for u in range(4):
         take_text_cross(u)
     weight = weights(other, slice(0, 256))
@@ -265,7 +276,7 @@
             if q:
                 back_i[p, q] = copy(ri1.at[p, q], ri1_in.at[p, q], dx=turn * ax, dy=turn * ay)
 
-    back_behind = [plane_back(behind + i) for i in (0, 1)]
+    back_behind = plane_back(behind)
     home_i = []
 
     def home_image(p):
@@ -281,13 +292,13 @@
             if IMAGE_Z[p][i]:
                 home_i.append(copy(ri2.at[p, i], ri2_in.at[p, i], dz=sign * IMAGE_Z[p][i]))
 
-    home_t += [home_text(ahead + i, back_ahead[i]) for i in (0, 1)]
+    home_t += home_text(ahead, back_ahead)
     for n in range(FEATS // 128):
         at = slice(128 * n, 128 * n + 128)
         wt_ref[:, at] = w_ref[at, :].T
     for p in (3, 2, 1, 0):
         home_image(p)
-    home_t += [home_text(behind + i, back_behind[i]) for i in (0, 1)]
+    home_t += home_text(behind, back_behind)
     drain()
 
     arrive(home_i)
@@ -353,8 +364,8 @@
             pltpu.VMEM((256, 128), half),
             pltpu.VMEM((128, D), jnp.float32),
             pltpu.VMEM((256, D), jnp.float32),
-            pltpu.VMEM((4, 4) + block, half),
-            pltpu.VMEM((4, 4) + block, half),
+            pltpu.VMEM((2, 4, 2 * D // 16, 128), half),
+            pltpu.VMEM((2, 4, 2 * D // 16, 128), half),
             pltpu.VMEM((4,) + block, half),
             pltpu.VMEM((4,) + block, half),
             pltpu.VMEM((4, 4, 2 * D // 16, 128), half),

time: 64.8 us -> 64.9 us (level)
  the two profiles are of different devices: /device:TPU:8 before, /device:TPU:2 now
where the time goes in v5:
time: 64.9 us; the launch traced here: 64.7 us
  Pallas kernels  61.6 us (95%)
  between operations  1.93 us (3%)
  local copies, waits for them, and re-layouts  1.22 us (2%)
    pallas_call x1, Pallas kernels, body(): pl.pallas_call(kernel, out_shape=(pltpu.VMEM((ROWS, FEATS), half), pltpu....  61.6 us

profile of v5, /device:TPU:2, one launch (start us, length us, event | category | flops | bytes accessed | tf_op | source)
XLA Modules:
  0.0 64.7 jit_solution(17921697738782051662)
XLA Ops:
  1.9 61.6 %contrast.1 = (bf16[8,1536]{1,0:T(8,128)(2,1)S(1)}, bf16[8,1152]{1,0:T(8,128)(2,1)S(1)}) custom-call(f32[1]{0:T(128)S(6)} %copy.14.scale_hbm, f32[1]{0:T(128)S(6)} %copy.15.offset_hbm, s32[8]{0:T(128)} %slot_hbm.1, s32[8]{0:T(128)} %iclass_hbm.1, s32[8]{0:T(128)} %tclass_hbm.1, bf16[8,1536]{1,0:T(8,128)(2,1)} %pooled_hbm.1, bf16[8,1152]{1,0:T(8,128)(2,1)} %caption_hbm.1, ...), custom_call_target="tpu_custom_call" | custom-call | tf_op jit(solution)/shard_map/contrast/pallas_call | solution.py:337
  63.5 0.6 copy.12
  64.1 0.6 copy.13
